TPU v7x, 256 devices: a whole 4x4x8 slice. The times are simulated.
256 devices in a mesh: gz: 128 (over y, x_lo, z, core), ta: 2 (over x_hi).
Axes of the slice: x: 4 (x_hi: 2, x_lo: 2; x = x_hi * 2 + x_lo), y: 4, z: 8, core: 2. Of those that a mesh axis runs over, the one named last changes fastest.
Arguments:
- field: bfloat16 [8, 128, 20, 128, 128], P('ta', 'gz'), may hold values from -6 to 6
- cotangent: bfloat16 [8, 128, 20, 128, 128], P('ta', 'gz'), may hold values from -6 to 6
- mix_weight: bfloat16 [20, 20], replicated, may hold values from -1.25 to 1.25
- bias: float32 [20], replicated, may hold values from -0.8 to 0.8
- spectral_weight: float32 [8, 16, 256, 20, 20], P('ta', None, 'gz'), may hold values from -6 to 6
Outputs:
- field_grad: bfloat16 [8, 128, 20, 128, 128], P('ta', 'gz')
- weight_grad: float32 [20, 20], replicated
- bias_grad: float32 [20], replicated
- spectral_grad: float32 [8, 16, 256, 20, 20], P('ta', None, 'gz')
All inputs are finite; a program needn't handle non-finite values.
Results may differ from a plain program's by a relative error of at most 0.012.
Values sent between devices are 32-bit elements; how exact they have to be, the bound alone decides.
A program may use at most 64 MiB of HBM per device.

v0:
```python
import math

import jax
import jax.numpy as jnp
import ml_dtypes
import numpy as np
from jax import lax
from jax.experimental import pallas as pl
from jax.experimental.pallas import tpu as pltpu
from jax.sharding import PartitionSpec as P

F32 = jnp.float32
BF16 = jnp.bfloat16
HIGHEST = lax.Precision.HIGHEST
MESH = pl.DeviceIdType.MESH

C = 20
CH = 10
CP = 16
NX = 128
NY = 128
NZ = 128
NT = 8
TD = 4
PLANES = TD * C
GROUPS = 2 * TD


def fourier_rows(length, kept):
    half = kept // 2
    frequency = np.concatenate([np.arange(half + 1), np.arange(1, kept - half)])
    angles = (frequency[:, None] * np.arange(length)[None, :] % length) * (2.0 * math.pi / length)
    waves = np.concatenate([np.cos(angles[: half + 1]), np.sin(angles[half + 1 :])], axis=0)
    return (waves * math.sqrt(2.0 / length)).astype(np.float32)


def two_parts(table):
    high = table.astype(ml_dtypes.bfloat16)
    return high, (table - high.astype(np.float32)).astype(ml_dtypes.bfloat16)


def tables():
    fx, fy = fourier_rows(NX, 16), fourier_rows(NY, 16)
    fz, ft = fourier_rows(NZ, 16), fourier_rows(NT, 8)
    y_fwd = np.zeros((CH, NY, 8, 2, CP), np.float32)
    y_back = np.zeros((8, 2, CP, CH, NY), np.float32)
    for k in range(CH):
        y_fwd[k, :, :, :, k] = fy.T.reshape(NY, 8, 2)
        y_back[:, :, k, k, :] = fy.reshape(8, 2, NY)
    y_fwd = y_fwd.reshape(CH * NY, 256).astype(ml_dtypes.bfloat16)
    yb_high, yb_low = two_parts(y_back.reshape(256, CH * NY))
    fx_high, fx_low = two_parts(fx)
    x_fwd = np.concatenate(
        [np.concatenate([fx_high, fx_high], 1), np.concatenate([fx_low, np.zeros_like(fx_low)], 1)], 0
    )
    x_back = np.concatenate([fx_high.T, fx_high.T, fx_low.T], 1)
    fz_high, fz_low = two_parts(fz)
    z_back = np.concatenate([fz_high.T, fz_high.T, fz_low.T], 1)
    z_fwd = np.repeat(fz, 2, axis=1)
    t_back = np.stack([np.kron(ft[TD * h : TD * h + TD], np.eye(32, dtype=np.float32)) for h in range(2)])
    return {
        "y_fwd": y_fwd, "x_fwd": x_fwd, "z_fwd": z_fwd, "t_fwd": ft, "t_back": t_back,
        "z_back": z_back, "yb_high": yb_high, "yb_low": yb_low, "x_back": x_back,
    }


def gelu_slope(v):
    size = jnp.abs(v)
    bell = jnp.exp(v * v * -0.5)
    d = 1.0 + 0.2316419 * size
    t = pl.reciprocal(d, approx=True)
    t = t * (2.0 - d * t)
    s = 0.3989422804014327
    tail = t * (0.319381530 * s + t * (-0.356563782 * s + t * (1.781477937 * s + t * (-1.821255978 * s + t * (1.330274429 * s)))))
    w = (tail - s * size) * bell
    return jnp.where(v < 0.0, w, 1.0 - w)


def split(values):
    high = values.astype(BF16)
    return high, (values - high.astype(F32)).astype(BF16)


def dot(a, b, precision=None):
    return jnp.dot(a, b, preferred_element_type=F32, precision=precision)


def main_kernel(
    field_h, cot_h, weight_h, mix, bias, t_fwd, x_fwd, z_fwd, z_back, x_back, y_fwd_h, t_back_h, yb_high_h, yb_low_h,
    lin_o, sg_o, cells_o, sums_o,
    field, cot, grad, lin, w_raw, w_t, sg_raw, y_fwd, t_back, yb_high, yb_low, xs, h_rows, mixed_s, mix_kron, acc,
    send1, send2, send3, send4, recv1, recv2, recv3, recv4, ring_s, ring_r, plane_s, plane_r,
    in_sem, w_sem, out_sem, sg_sem, send_sem, recv_sem, small_send, small_recv,
):
    gz, ta = lax.axis_index("gz"), lax.axis_index("ta")
    core = lax.rem(gz, 2)
    z = lax.rem(gz // 2, 8)
    x = ta * 2 + lax.rem(gz // 16, 2)
    y = gz // 32
    me = gz * 2 + ta

    def load(k, src, dst):
        return pltpu.make_async_copy(src, dst, in_sem.at[k])

    field_in = [load(t, field_h.at[pl.ds(t * C, C)], field.at[pl.ds(t * C, C)]) for t in range(TD)]
    rest_in = [
        load(5, cot_h, cot), load(6, t_back_h, t_back), load(7, yb_high_h, yb_high), load(8, yb_low_h, yb_low),
    ]
    table_in = load(4, y_fwd_h, y_fwd)
    w_in = [
        pltpu.make_async_copy(weight_h.at[f, :, b], w_raw.at[pl.ds((f * 2 + b) * 16, 16)], w_sem.at[f * 2 + b])
        for f in range(TD)
        for b in range(2)
    ]
    table_in.start()
    for copy in field_in + w_in + rest_in:
        copy.start()

    barrier = pltpu.get_barrier_semaphore()

    def each_peer(do):
        def step(k, _):
            kz, ky, kx = k // 16, lax.rem(k // 4, 4), lax.rem(k, 4)
            dz = 4 + ((kz + 1) // 2) * (1 - 2 * lax.rem(kz, 2))
            dy = 2 + ((ky + 1) // 2) * (1 - 2 * lax.rem(ky, 2))
            dx = 2 + ((kx + 1) // 2) * (1 - 2 * lax.rem(kx, 2))
            pz, py, px = lax.rem(z + dz, 8), lax.rem(y + dy, 4), lax.rem(x + dx, 4)
            g = py * 32 + lax.rem(px, 2) * 16 + pz * 2
            t = px // 2
            do(g + core, t)
            do(g + 1 - core, t)
            return 0

        lax.fori_loop(0, 127, step, 0)
        do(gz + 1 - 2 * core, ta)

    def greet(g, t):
        pl.semaphore_signal(barrier, inc=1, device_id=(g, t), device_id_type=MESH)

    def exchange(k, source, target):
        pltpu.make_async_copy(source(gz, ta), target, recv_sem.at[k]).start()

        def send(g, t):
            pltpu.make_async_remote_copy(
                src_ref=source(g, t), dst_ref=target, send_sem=send_sem.at[k], recv_sem=recv_sem.at[k],
                device_id=(g, t), device_id_type=MESH,
            ).start()

        each_peer(send)

    def arrived(k, whole):
        pltpu.make_async_copy(whole, whole, recv_sem.at[k]).wait()

    def by_mode(buffer):
        return lambda g, t: buffer.at[g // 8, lax.rem(g, 8) * 2 + t]

    def by_cell(buffer):
        return lambda g, t: buffer.at[g, t]

    def plane_modes(k, planes):
        lhs = jnp.concatenate(planes, axis=1)
        high, low = split(dot(lhs, y_fwd[...]))
        both = dot(x_fwd[...], jnp.concatenate([high, low], axis=0))
        xs[k] = both[:16] + both[16:]

    def mode_messages(send):
        parts = [xs[k] for k in range(GROUPS)]
        for h in range(2):
            mixed = []
            for f in range(TD):
                c = [t_fwd[h * TD + f, ta * TD + t] for t in range(TD)]
                for half in range(2):
                    mixed.append(sum(c[t] * parts[t * 2 + half] for t in range(TD)))
            for r in range(8):
                for j in range(2):
                    send[:, r * 2 + h, j, :] = jnp.concatenate(
                        [mixed[4 * j + i][:, r * 32 : r * 32 + 32] for i in range(4)], axis=1
                    )

    def spectrum(recv):
        flat = [jnp.transpose(dot(z_fwd[...], recv[:, j, :], HIGHEST)) for j in range(2)]
        blocks = []
        for f in range(TD):
            for b in range(2):
                rows = [((f % 2) * 4 + half * 2 + b) * 16 for half in range(2)]
                blocks.append(jnp.concatenate([flat[f // 2][r : r + 16] for r in rows], axis=0))
        return jnp.concatenate(blocks, axis=1)

    def cell_messages(modes, send):
        steps = jnp.transpose(dot(modes, t_back[ta], HIGHEST))
        pieces = []
        for t in range(NT):
            for half in range(2):
                for b in range(2):
                    row = (t * 2 + b) * 16
                    pieces.append(steps[row : row + 16, half * CP : half * CP + CP])
        high, low = split(jnp.concatenate(pieces, axis=1))
        cells = dot(z_back[...], jnp.concatenate([high, low, high], axis=0))
        for k in range(4):
            send[:, k // 2, k % 2, :] = cells[:, k * 128 : k * 128 + 128]

    def cell_rows(recv, out):
        rows = [[recv[:, 2 * r, j, :] + recv[:, 2 * r + 1, j, :] for j in range(2)] for r in range(8)]
        groups = []
        for k in range(GROUPS):
            at = (k % 4) * 32
            groups.append(jnp.concatenate([rows[r][k // 4][:, at : at + 32] for r in range(8)], axis=1))
        high, low = split(jnp.concatenate(groups, axis=0))
        both = jnp.concatenate([high, low], axis=0)
        for n in range(5):
            cut = slice(n * 256, n * 256 + 256)
            wide = dot(both, yb_high[:, cut])
            values = wide[:128] + wide[128:] + dot(high, yb_low[:, cut])
            top, rest = split(values)
            for k in range(GROUPS):
                out[k, 0:16, cut] = top[k * 16 : k * 16 + 16]
                out[k, 16:32, cut] = rest[k * 16 : k * 16 + 16]
                out[k, 32:48, cut] = top[k * 16 : k * 16 + 16]

    def tile_rows(source, t, xt):
        at = pl.multiple_of(xt * 16, 16)
        return source[pl.ds(t * C, C), pl.ds(at, 16), :].reshape(C * 16, NY)

    def pair_rows(source, pair, xt):
        return jnp.concatenate([tile_rows(source, pair * 2, xt), tile_rows(source, pair * 2 + 1, xt)], axis=1)

    def make_kron(transposed):
        pick = (lax.broadcasted_iota(jnp.int32, (C * 16, C), 0) // 16 == lax.broadcasted_iota(jnp.int32, (C * 16, C), 1)).astype(BF16)
        dims = (((1,), (1 if transposed else 0,)), ((), ()))
        tall = lax.dot_general(pick, mix[...], dims, preferred_element_type=F32).astype(BF16)
        wide = lax.dot_general(tall, pick, (((1,), (1,)), ((), ())), preferred_element_type=F32)
        same = lax.rem(lax.broadcasted_iota(jnp.int32, wide.shape, 0), 16) == lax.rem(lax.broadcasted_iota(jnp.int32, wide.shape, 1), 16)
        mix_kron[...] = jnp.where(same, wide, 0.0).astype(BF16)

    def channel_mix(source, add_bias):
        def step(k, _):
            pair, xt = lax.rem(k, 2), k // 2
            out = dot(mix_kron[...], pair_rows(source, pair, xt))
            at = pl.multiple_of(xt * 16, 16)
            for i in range(2):
                for o in range(C):
                    part = out[o * 16 : o * 16 + 16, i * 128 : i * 128 + 128]
                    lin[(pair * 2 + i) * C + o, pl.ds(at, 16), :] = part + bias[o] if add_bias else part
            return 0

        lax.fori_loop(0, 16, step, 0)

    each_peer(greet)
    table_in.wait()
    for t in range(TD):
        field_in[t].wait()

    def field_step(k, _):
        plane_modes(k, [field[k * CH + i] for i in range(CH)])
        return 0

    lax.fori_loop(0, GROUPS, field_step, 0)
    mode_messages(send1)
    pl.semaphore_wait(barrier, 255)
    exchange(0, by_mode(send1), recv1.at[me])
    make_kron(False)
    channel_mix(field, True)
    for copy in w_in + rest_in:
        copy.wait()
    w_t[...] = jnp.zeros_like(w_t)
    for o in range(C):
        turned = jnp.transpose(w_raw[:, o, :])
        w_t[o, 0:CH, :] = turned[:CH]
        w_t[o, CP : CP + CH, :] = turned[CH:]
    mixed_s[...] = jnp.zeros_like(mixed_s)
    arrived(0, recv1)
    field_spec = spectrum(recv1)
    for o in range(C):
        row = o if o < CH else o - CH + CP
        mixed_s[row : row + 1, :] = jnp.sum(w_t[o] * field_spec, axis=0, keepdims=True)
    cell_messages(mixed_s[...], send2)
    exchange(1, by_cell(send2), recv2.at[gz // 8, lax.rem(gz, 8) * 2 + ta])
    make_kron(True)
    acc[...] = jnp.zeros_like(acc)
    arrived(1, recv2)
    cell_rows(recv2, h_rows)

    def grad_step(k, _):
        planes = []
        for n in range(5):
            pair = dot(x_back[...], h_rows[k, :, n * 256 : n * 256 + 256])
            for i in range(2):
                p = k * CH + n * 2 + i
                slope = gelu_slope(lin[p] + pair[:, i * 128 : i * 128 + 128])
                value = (cot[p].astype(F32) * slope).astype(BF16)
                grad[p] = value
                planes.append(value)
        plane_modes(k, planes)
        return 0

    lax.fori_loop(0, GROUPS, grad_step, 0)
    mode_messages(send3)
    exchange(2, by_mode(send3), recv3.at[me])

    def sum_step(k, _):
        pair, xt = lax.rem(k, 2), k // 2
        left = jnp.concatenate([pair_rows(field, pair, xt), jnp.ones((16, 256), BF16)], axis=0)
        acc[...] += lax.dot_general(
            left, pair_rows(grad, pair, xt), (((1,), (1,)), ((), ())), preferred_element_type=F32
        )
        return 0

    lax.fori_loop(0, 16, sum_step, 0)
    shape = acc.shape
    same = lax.rem(lax.broadcasted_iota(jnp.int32, shape, 0), 16) == lax.rem(lax.broadcasted_iota(jnp.int32, shape, 1), 16)
    kept = jnp.where(same, acc[...], 0.0)
    rows = (lax.broadcasted_iota(jnp.int32, (24, shape[0]), 1) // 16 == lax.broadcasted_iota(jnp.int32, (24, shape[0]), 0)).astype(F32)
    lanes = (lax.broadcasted_iota(jnp.int32, (shape[1], 32), 0) // 16 == lax.broadcasted_iota(jnp.int32, (shape[1], 32), 1)).astype(F32)
    sums = dot(dot(rows, kept, HIGHEST), lanes, HIGHEST)
    ring_s[...] = jnp.concatenate([sums[0:8], sums[8:16], sums[16:24], jnp.zeros((8, 32), F32)], axis=1)
    p, q = gz // 16, lax.rem(gz, 16)

    def small(k, source, target, peer):
        return pltpu.make_async_remote_copy(
            src_ref=source, dst_ref=target, send_sem=small_send.at[k], recv_sem=small_recv.at[k],
            device_id=peer, device_id_type=MESH,
        )

    pltpu.make_async_copy(ring_s, ring_r.at[q], small_recv.at[0]).start()

    def ring_step(d, _):
        small(0, ring_s, ring_r.at[q], (p * 16 + lax.rem(q + d, 16), ta)).start()
        return 0

    lax.fori_loop(1, 16, ring_step, 0)
    channel_mix(grad, False)
    lin_out = pltpu.make_async_copy(lin, lin_o, out_sem.at[0])
    lin_out.start()
    arrived(2, recv3)
    grad_spec = spectrum(recv3)
    back = jnp.zeros((32, 128), F32)
    for o in range(C):
        row = o if o < CH else o - CH + CP
        back = back + w_t[o] * grad_spec[row : row + 1]
    cell_messages(back, send4)
    exchange(3, by_cell(send4), recv4.at[gz // 8, lax.rem(gz, 8) * 2 + ta])
    pltpu.make_async_copy(ring_r, ring_r, small_recv.at[0]).wait()
    total = ring_r[0]
    for i in range(1, 16):
        total = total + ring_r[i]
    plane_s[...] = total
    v = p * 2 + ta
    pltpu.make_async_copy(plane_s, plane_r.at[v], small_recv.at[1]).start()

    def plane_step(d, _):
        u = lax.rem(v + d, 16)
        small(1, plane_s, plane_r.at[v], ((u // 2) * 16 + q, lax.rem(u, 2))).start()
        return 0

    lax.fori_loop(1, 16, plane_step, 0)
    for o in range(C):
        row = o if o < CH else o - CH + CP
        turned = jnp.transpose(field_spec * grad_spec[row : row + 1])
        sg_raw[:, o, :] = jnp.concatenate([turned[:, :CH], turned[:, CP : CP + CH]], axis=1)
    sg_out = [
        pltpu.make_async_copy(sg_raw.at[pl.ds((f * 2 + b) * 16, 16)], sg_o.at[f, :, b], sg_sem.at[f * 2 + b])
        for f in range(TD)
        for b in range(2)
    ]
    for copy in sg_out:
        copy.start()
    arrived(3, recv4)
    cell_rows(recv4, cells_o)
    pltpu.make_async_copy(plane_r, plane_r, small_recv.at[1]).wait()
    total = plane_r[0]
    for i in range(1, 16):
        total = total + plane_r[i]
    sums_o[...] = total
    for copy in sg_out:
        copy.wait()
    lin_out.wait()
    for k in range(4):
        sent = recv1.at[pl.ds(0, 255)]
        pltpu.make_async_copy(sent, sent, send_sem.at[k]).wait()
    for k in range(2):
        sent = ring_r.at[pl.ds(0, 15)]
        pltpu.make_async_copy(sent, sent, small_send.at[k]).wait()


def last_kernel(lin, cells, x_back, sums, sg_in, out, wg, bg, sg_out, sem):
    k = pl.program_id(0)
    copy = pltpu.make_async_copy(sg_in, sg_out, sem)

    @pl.when(k == 0)
    def _():
        copy.start()
        scale = 1.0 / math.sqrt(NX * NY * NZ * NT)
        rows = jnp.concatenate([sums[:, 32 * i : 32 * i + 32] for i in range(3)], axis=0) * scale
        wg[...] = jnp.transpose(rows)[:C, :C]
        bg[...] = rows[C : C + 1, :C]

    for n in range(5):
        pair = dot(x_back[...], cells[0, :, n * 256 : n * 256 + 256])
        for i in range(2):
            out[n * 2 + i] = (lin[n * 2 + i] + pair[:, i * 128 : i * 128 + 128]).astype(BF16)

    @pl.when(k == pl.num_programs(0) - 1)
    def _():
        copy.wait()


def per_device(field, cotangent, mix_weight, bias, spectral_weight):
    tab = tables()
    shape = field.shape
    planes = (PLANES, NX, NY)
    any_, vmem, smem = (pl.BlockSpec(memory_space=m) for m in (pl.ANY, pltpu.VMEM, pltpu.SMEM))
    dma = pltpu.SemaphoreType.DMA
    sent, cells = pltpu.VMEM((16, 16, 2, 128), F32), pltpu.VMEM((128, 2, 2, 128), F32)
    rows = pltpu.VMEM((256, 2, 128), F32)
    small = pltpu.VMEM((16, 8, 128), F32)
    lin, sg, h_rows, sums = pl.pallas_call(
        main_kernel,
        out_shape=(
            jax.ShapeDtypeStruct(planes, F32),
            jax.ShapeDtypeStruct(spectral_weight.shape, F32),
            jax.ShapeDtypeStruct((GROUPS, 48, CH * NY), BF16),
            jax.ShapeDtypeStruct((8, 128), F32),
        ),
        in_specs=[any_, any_, any_, vmem, smem, smem, vmem, vmem, vmem, vmem, any_, any_, any_, any_],
        out_specs=(any_, any_, vmem, vmem),
        scratch_shapes=[
            pltpu.VMEM(planes, BF16), pltpu.VMEM(planes, BF16), pltpu.VMEM(planes, BF16), pltpu.VMEM(planes, F32),
            pltpu.VMEM((128, C, C), F32), pltpu.VMEM((C, 32, 128), F32), pltpu.VMEM((128, C, C), F32),
            pltpu.VMEM((CH * NY, 256), BF16), pltpu.VMEM((2, 128, 256), F32),
            pltpu.VMEM((256, CH * NY), BF16), pltpu.VMEM((256, CH * NY), BF16),
            pltpu.VMEM((GROUPS, 16, 256), F32), pltpu.VMEM((GROUPS, 48, CH * NY), BF16), pltpu.VMEM((32, 128), F32),
            pltpu.VMEM((C * 16, C * 16), BF16), pltpu.VMEM((C * 16 + 16, C * 16), F32),
            sent, cells, sent, cells, rows, sent, rows, sent,
            pltpu.VMEM((8, 128), F32), small, pltpu.VMEM((8, 128), F32), small,
            dma((9,)), dma((8,)), dma((1,)), dma((8,)), dma((4,)), dma((4,)), dma((2,)), dma((2,)),
        ],
        compiler_params=pltpu.CompilerParams(collective_id=0, has_side_effects=True, vmem_limit_bytes=56 * 2**20),
    )(
        field.reshape(planes), cotangent.reshape(planes), spectral_weight, mix_weight, bias,
        tab["t_fwd"], tab["x_fwd"], tab["z_fwd"], tab["z_back"], tab["x_back"],
        tab["y_fwd"], tab["t_back"], tab["yb_high"], tab["yb_low"],
    )
    whole = lambda *dims: pl.BlockSpec(dims, lambda k: (0,) * len(dims))
    field_grad, wg, bg, sg = pl.pallas_call(
        last_kernel,
        grid=(GROUPS,),
        out_shape=(
            jax.ShapeDtypeStruct(planes, BF16),
            jax.ShapeDtypeStruct((C, C), F32),
            jax.ShapeDtypeStruct((1, C), F32),
            jax.ShapeDtypeStruct(spectral_weight.shape, F32),
        ),
        in_specs=[
            pl.BlockSpec((CH, NX, NY), lambda k: (k, 0, 0)),
            pl.BlockSpec((1, 48, CH * NY), lambda k: (k, 0, 0)),
            whole(NX, 48), whole(8, 128), any_,
        ],
        out_specs=(pl.BlockSpec((CH, NX, NY), lambda k: (k, 0, 0)), whole(C, C), whole(1, C), any_),
        scratch_shapes=[dma(())],
        compiler_params=pltpu.CompilerParams(vmem_limit_bytes=32 * 2**20),
    )(lin, h_rows, tab["x_back"], sums, sg)
    return field_grad.reshape(shape), wg, bg.reshape(C), sg


def solution(mesh):
    return jax.shard_map(
        per_device,
        mesh=mesh,
        in_specs=(
            P("ta", "gz", None, None, None),
            P("ta", "gz", None, None, None),
            P(),
            P(),
            P("ta", None, "gz", None, None),
        ),
        out_specs=(P("ta", "gz", None, None, None), P(), P(), P("ta", None, "gz", None, None)),
        check_vma=False,
    )
```

profile of v0, /device:TPU:1, one launch (start us, length us, event | category | flops | bytes accessed | tf_op | source)
XLA Modules:
  0.0 102.6 jit_solution(11781291587853604182)
XLA Ops:
  0.6 2.6 %copy.18.weight_h = f32[4,16,2,20,20]{4,3,2,1,0:T(8,128)} copy(f32[4,16,2,20,20]{4,2,3,1,0:T(2,128)} %param.18) | data formatting | bytes 409600 | tf_op args[4]
  3.3 0.0 copy-start.3
  3.3 87.5 %shard_map.165 = (f32[80,128,128]{2,1,0:T(8,128)}, f32[4,16,2,20,20]{4,3,2,1,0:T(8,128)}, bf16[8,48,1280]{2,1,0:T(8,128)(2,1)}, f32[8,128]{1,0:T(8,128)}) custom-call(bf16[80,128,128]{2,1,0:T(8,128)(2,1)} %bitcast.6, bf16[80,128,128]{2,1,0:T(8,128)(2,1)} %bitcast.7, f32[4,16,2,20,20]{4,3,2,1,0:T(8,128)} %copy.18.weight_h, bf16[20,20]{1,0:T(8,128)(2,1)} %mix.1, ...), custom_call_target="tpu_custom_call" | custom-call | tf_op jit(solution)/shard_map/pallas_call | solution.py:416
  90.8 0.0 copy-done.3
  90.8 0.0 copy-start
  90.8 2.5 %copy-done = f32[80,128,128]{2,1,0:T(8,128)S(1)} copy-done((f32[80,128,128]{2,1,0:T(8,128)S(1)}, f32[80,128,128]{2,1,0:T(8,128)}, u32[]{:S(2)}) %copy-start) | copy-done | bytes 5242904
  93.3 0.0 copy-start.1
  93.3 1.4 %copy-done.1 = f32[4,16,2,20,20]{4,3,2,1,0:T(8,128)S(1)} copy-done((f32[4,16,2,20,20]{4,3,2,1,0:T(8,128)S(1)}, f32[4,16,2,20,20]{4,3,2,1,0:T(8,128)}, u32[]{:S(2)}) %copy-start.1) | copy-done | bytes 204824
  94.7 0.0 copy-start.2
  94.7 1.2 %copy-done.2 = bf16[8,48,1280]{2,1,0:T(8,128)(2,1)S(1)} copy-done((bf16[8,48,1280]{2,1,0:T(8,128)(2,1)S(1)}, bf16[8,48,1280]{2,1,0:T(8,128)(2,1)}, u32[]{:S(2)}) %copy-start.2) | copy-done | bytes 983064
  95.9 0.0 copy-start.4
  95.9 0.7 copy-done.4
  96.5 4.3 %shard_map.166 = (bf16[80,128,128]{2,1,0:T(8,128)(2,1)}, f32[20,20]{1,0:T(8,128)}, f32[1,20]{1,0:T(1,128)}, f32[4,16,2,20,20]{4,3,2,1,0:T(8,128)S(1)}) custom-call(f32[80,128,128]{2,1,0:T(8,128)S(1)} %copy-done, bf16[8,48,1280]{2,1,0:T(8,128)(2,1)S(1)} %copy-done.2, bf16[128,48]{1,0:T(8,128)(2,1)S(1)} %copy-done.3, f32[8,128]{1,0:T(8,128)S(1)} %copy-done.4, ...), custom_call_target="tpu_custom_call" | custom-call | tf_op jit(solution)/shard_map/pallas_call | solution.py:444
  100.9 1.7 %copy.20 = f32[4,16,2,20,20]{4,2,3,1,0:T(2,128)} copy(f32[4,16,2,20,20]{4,3,2,1,0:T(8,128)S(1)} %get-tuple-element.23) | data formatting | bytes 409600
Async XLA Ops:
  3.3 87.5 %copy-start.3 = (bf16[128,48]{1,0:T(8,128)(2,1)S(1)}, bf16[128,48]{1,0:T(8,128)(2,1)}, u32[]{:S(2)}) copy-start(bf16[128,48]{1,0:T(8,128)(2,1)} %constant.19.clone.z_back.x_back) | copy-start | bytes 36868
  90.8 2.5 %copy-start = (f32[80,128,128]{2,1,0:T(8,128)S(1)}, f32[80,128,128]{2,1,0:T(8,128)}, u32[]{:S(2)}) copy-start(f32[80,128,128]{2,1,0:T(8,128)} %get-tuple-element.12.lin) | copy-start | bytes 15728644
  93.3 1.4 %copy-start.1 = (f32[4,16,2,20,20]{4,3,2,1,0:T(8,128)S(1)}, f32[4,16,2,20,20]{4,3,2,1,0:T(8,128)}, u32[]{:S(2)}) copy-start(f32[4,16,2,20,20]{4,3,2,1,0:T(8,128)} %get-tuple-element.15.sg_in) | copy-start | bytes 614404
  94.7 1.2 %copy-start.2 = (bf16[8,48,1280]{2,1,0:T(8,128)(2,1)S(1)}, bf16[8,48,1280]{2,1,0:T(8,128)(2,1)}, u32[]{:S(2)}) copy-start(bf16[8,48,1280]{2,1,0:T(8,128)(2,1)} %get-tuple-element.13.cells) | copy-start | bytes 2949124
  95.9 0.7 copy-start.4
where the time goes:
time: 103 us
  Pallas kernels  91.8 us (89%)
  local copies, waits for them, and re-layouts  10.1 us (10%)
    pallas_call x1, Pallas kernels, per_device(): pl.pallas_call(main_kernel, out_shape=(jax.ShapeDtypeStruct(planes, F32),...  87.5 us
    unnamed x12, local copies, waits for them, and re-layouts  10.1 us
    pallas_call x1, Pallas kernels, per_device(): pl.pallas_call(last_kernel, grid=(GROUPS,), out_shape=(jax.ShapeDtypeStru...  4.31 us

commit v1 on v0

--- a/solution.py
+++ b/solution.py
@@ -57,7 +57,8 @@
     fz_high, fz_low = two_parts(fz)
     z_back = np.concatenate([fz_high.T, fz_high.T, fz_low.T], 1)
     z_fwd = np.repeat(fz, 2, axis=1)
-    t_back = np.stack([np.kron(ft[TD * h : TD * h + TD], np.eye(32, dtype=np.float32)) for h in range(2)])
+    t_back = np.einsum("hft,bB,eE->hbfetBE", ft.reshape(2, TD, NT), np.eye(2), np.eye(16))
+    t_back = t_back.reshape(2, 128, 256).astype(np.float32)
     return {
         "y_fwd": y_fwd, "x_fwd": x_fwd, "z_fwd": z_fwd, "t_fwd": ft, "t_back": t_back,
         "z_back": z_back, "yb_high": yb_high, "yb_low": yb_low, "x_back": x_back,
@@ -86,9 +87,9 @@
 
 
 def main_kernel(
-    field_h, cot_h, weight_h, mix, bias, t_fwd, x_fwd, z_fwd, z_back, x_back, y_fwd_h, t_back_h, yb_high_h, yb_low_h,
+    field_h, cot_h, weight_h, mix_h, bias, t_fwd, x_fwd_h, z_fwd_h, z_back_h, x_back_h, y_fwd_h, t_back_h, yb_high_h, yb_low_h,
     lin_o, sg_o, cells_o, sums_o,
-    field, cot, grad, lin, w_raw, w_t, sg_raw, y_fwd, t_back, yb_high, yb_low, xs, h_rows, mixed_s, mix_kron, acc,
+    field, cot, grad, lin, w_raw, w_t, sg_raw, mix, x_fwd, z_fwd, z_back, x_back, y_fwd, t_back, yb_high, yb_low, xs, h_rows, mixed_s, mix_kron, acc,
     send1, send2, send3, send4, recv1, recv2, recv3, recv4, ring_s, ring_r, plane_s, plane_r,
     in_sem, w_sem, out_sem, sg_sem, send_sem, recv_sem, small_send, small_recv,
 ):
@@ -105,45 +106,43 @@
     field_in = [load(t, field_h.at[pl.ds(t * C, C)], field.at[pl.ds(t * C, C)]) for t in range(TD)]
     rest_in = [
         load(5, cot_h, cot), load(6, t_back_h, t_back), load(7, yb_high_h, yb_high), load(8, yb_low_h, yb_low),
+        load(10, mix_h, mix), load(11, z_fwd_h, z_fwd), load(12, z_back_h, z_back), load(13, x_back_h, x_back),
     ]
-    table_in = load(4, y_fwd_h, y_fwd)
-    w_in = [
-        pltpu.make_async_copy(weight_h.at[f, :, b], w_raw.at[pl.ds((f * 2 + b) * 16, 16)], w_sem.at[f * 2 + b])
-        for f in range(TD)
-        for b in range(2)
-    ]
-    table_in.start()
-    for copy in field_in + w_in + rest_in:
+    table_in = [load(4, y_fwd_h, y_fwd), load(9, x_fwd_h, x_fwd)]
+    w_in = [pltpu.make_async_copy(weight_h, w_raw, w_sem.at[0])]
+    for copy in table_in + field_in + w_in + rest_in:
         copy.start()
 
     barrier = pltpu.get_barrier_semaphore()
 
+    steps = sorted(((dy, dx) for dy in range(4) for dx in range(4)), key=lambda d: -(min(d[0], 4 - d[0]) + min(d[1], 4 - d[1])))
+    ys, xs_ = [lax.rem(y + d, 4) for d in range(4)], [lax.rem(x + d, 4) for d in range(4)]
+    plane = [(ys[dy] * 2 + lax.rem(xs_[dx], 2), xs_[dx] // 2) for dy, dx in steps]
+
     def each_peer(do):
-        def step(k, _):
-            kz, ky, kx = k // 16, lax.rem(k // 4, 4), lax.rem(k, 4)
-            dz = 4 + ((kz + 1) // 2) * (1 - 2 * lax.rem(kz, 2))
-            dy = 2 + ((ky + 1) // 2) * (1 - 2 * lax.rem(ky, 2))
-            dx = 2 + ((kx + 1) // 2) * (1 - 2 * lax.rem(kx, 2))
-            pz, py, px = lax.rem(z + dz, 8), lax.rem(y + dy, 4), lax.rem(x + dx, 4)
-            g = py * 32 + lax.rem(px, 2) * 16 + pz * 2
-            t = px // 2
-            do(g + core, t)
-            do(g + 1 - core, t)
+        def step(kz, _):
+            pz = lax.rem(z + 4 + ((kz + 1) // 2) * (1 - 2 * lax.rem(kz, 2)), 8)
+            for p, t in plane:
+                do(p, pz, core, t)
+                do(p, pz, 1 - core, t)
             return 0
 
-        lax.fori_loop(0, 127, step, 0)
-        do(gz + 1 - 2 * core, ta)
-
-    def greet(g, t):
-        pl.semaphore_signal(barrier, inc=1, device_id=(g, t), device_id_type=MESH)
+        lax.fori_loop(0, 7, step, 0)
+        for p, t in plane[:-1]:
+            do(p, z, core, t)
+            do(p, z, 1 - core, t)
+        do(*plane[-1][:1], z, 1 - core, ta)
+
+    def greet(p, pz, c, t):
+        pl.semaphore_signal(barrier, inc=1, device_id=(p * 16 + pz * 2 + c, t), device_id_type=MESH)
 
     def exchange(k, source, target):
-        pltpu.make_async_copy(source(gz, ta), target, recv_sem.at[k]).start()
-
-        def send(g, t):
+        pltpu.make_async_copy(source(gz // 16, z, core, ta), target, recv_sem.at[k]).start()
+
+        def send(p, pz, c, t):
             pltpu.make_async_remote_copy(
-                src_ref=source(g, t), dst_ref=target, send_sem=send_sem.at[k], recv_sem=recv_sem.at[k],
-                device_id=(g, t), device_id_type=MESH,
+                src_ref=source(p, pz, c, t), dst_ref=target, send_sem=send_sem.at[k], recv_sem=recv_sem.at[k],
+                device_id=(p * 16 + pz * 2 + c, t), device_id_type=MESH,
             ).start()
 
         each_peer(send)
@@ -152,10 +151,10 @@
         pltpu.make_async_copy(whole, whole, recv_sem.at[k]).wait()
 
     def by_mode(buffer):
-        return lambda g, t: buffer.at[g // 8, lax.rem(g, 8) * 2 + t]
+        return lambda p, pz, c, t: buffer.at[p * 2 + pz // 4, lax.rem(pz, 4) * 4 + c * 2 + t]
 
     def by_cell(buffer):
-        return lambda g, t: buffer.at[g, t]
+        return lambda p, pz, c, t: buffer.at[p * 16 + pz * 2 + c, t]
 
     def plane_modes(k, planes):
         lhs = jnp.concatenate(planes, axis=1)
@@ -180,8 +179,8 @@
     def spectrum(recv):
         flat = [jnp.transpose(dot(z_fwd[...], recv[:, j, :], HIGHEST)) for j in range(2)]
         blocks = []
-        for f in range(TD):
-            for b in range(2):
+        for b in range(2):
+            for f in range(TD):
                 rows = [((f % 2) * 4 + half * 2 + b) * 16 for half in range(2)]
                 blocks.append(jnp.concatenate([flat[f // 2][r : r + 16] for r in rows], axis=0))
         return jnp.concatenate(blocks, axis=1)
@@ -246,9 +245,8 @@
         lax.fori_loop(0, 16, step, 0)
 
     each_peer(greet)
-    table_in.wait()
-    for t in range(TD):
-        field_in[t].wait()
+    for copy in table_in + field_in:
+        copy.wait()
 
     def field_step(k, _):
         plane_modes(k, [field[k * CH + i] for i in range(CH)])
@@ -258,13 +256,13 @@
     mode_messages(send1)
     pl.semaphore_wait(barrier, 255)
     exchange(0, by_mode(send1), recv1.at[me])
+    for copy in rest_in + w_in:
+        copy.wait()
     make_kron(False)
     channel_mix(field, True)
-    for copy in w_in + rest_in:
-        copy.wait()
     w_t[...] = jnp.zeros_like(w_t)
     for o in range(C):
-        turned = jnp.transpose(w_raw[:, o, :])
+        turned = jnp.transpose(jnp.concatenate([w_raw[:, o, b, :] for b in range(2)], axis=0))
         w_t[o, 0:CH, :] = turned[:CH]
         w_t[o, CP : CP + CH, :] = turned[CH:]
     mixed_s[...] = jnp.zeros_like(mixed_s)
@@ -328,9 +326,6 @@
         return 0
 
     lax.fori_loop(1, 16, ring_step, 0)
-    channel_mix(grad, False)
-    lin_out = pltpu.make_async_copy(lin, lin_o, out_sem.at[0])
-    lin_out.start()
     arrived(2, recv3)
     grad_spec = spectrum(recv3)
     back = jnp.zeros((32, 128), F32)
@@ -356,14 +351,15 @@
     for o in range(C):
         row = o if o < CH else o - CH + CP
         turned = jnp.transpose(field_spec * grad_spec[row : row + 1])
-        sg_raw[:, o, :] = jnp.concatenate([turned[:, :CH], turned[:, CP : CP + CH]], axis=1)
-    sg_out = [
-        pltpu.make_async_copy(sg_raw.at[pl.ds((f * 2 + b) * 16, 16)], sg_o.at[f, :, b], sg_sem.at[f * 2 + b])
-        for f in range(TD)
-        for b in range(2)
-    ]
+        for b in range(2):
+            part = turned[b * 64 : b * 64 + 64]
+            sg_raw[:, o, b, :] = jnp.concatenate([part[:, :CH], part[:, CP : CP + CH]], axis=1)
+    sg_out = [pltpu.make_async_copy(sg_raw, sg_o, sg_sem.at[0])]
     for copy in sg_out:
         copy.start()
+    channel_mix(grad, False)
+    lin_out = pltpu.make_async_copy(lin, lin_o, out_sem.at[0])
+    lin_out.start()
     arrived(3, recv4)
     cell_rows(recv4, cells_o)
     pltpu.make_async_copy(plane_r, plane_r, small_recv.at[1]).wait()
@@ -382,33 +378,44 @@
         pltpu.make_async_copy(sent, sent, small_send.at[k]).wait()
 
 
-def last_kernel(lin, cells, x_back, sums, sg_in, out, wg, bg, sg_out, sem):
+def last_kernel(lin, cells, x_back, sums, sg_in, out, wg, bg, sg_out, staged, sem):
     k = pl.program_id(0)
-    copy = pltpu.make_async_copy(sg_in, sg_out, sem)
+    copy_in = pltpu.make_async_copy(sg_in, staged, sem.at[0])
+    copy_out = pltpu.make_async_copy(staged, sg_out, sem.at[1])
 
     @pl.when(k == 0)
     def _():
-        copy.start()
+        copy_in.start()
         scale = 1.0 / math.sqrt(NX * NY * NZ * NT)
         rows = jnp.concatenate([sums[:, 32 * i : 32 * i + 32] for i in range(3)], axis=0) * scale
         wg[...] = jnp.transpose(rows)[:C, :C]
         bg[...] = rows[C : C + 1, :C]
 
-    for n in range(5):
-        pair = dot(x_back[...], cells[0, :, n * 256 : n * 256 + 256])
-        for i in range(2):
-            out[n * 2 + i] = (lin[n * 2 + i] + pair[:, i * 128 : i * 128 + 128]).astype(BF16)
+    for half in range(2):
+        for n in range(5):
+            pair = dot(x_back[...], cells[half, :, n * 256 : n * 256 + 256])
+            for i in range(2):
+                p = half * CH + n * 2 + i
+                out[p] = (lin[p] + pair[:, i * 128 : i * 128 + 128]).astype(BF16)
+
+    @pl.when(k == 1)
+    def _():
+        copy_in.wait()
+        copy_out.start()
 
     @pl.when(k == pl.num_programs(0) - 1)
     def _():
-        copy.wait()
+        copy_out.wait()
 
 
 def per_device(field, cotangent, mix_weight, bias, spectral_weight):
     tab = tables()
     shape = field.shape
     planes = (PLANES, NX, NY)
-    any_, vmem, smem = (pl.BlockSpec(memory_space=m) for m in (pl.ANY, pltpu.VMEM, pltpu.SMEM))
+    weight = jnp.transpose(spectral_weight, (0, 1, 3, 2, 4)).reshape(64, C, 2, C)
+    modes = (64, C, 2, C)
+    whole = lambda *dims: pl.BlockSpec(dims, lambda k: (0,) * len(dims))
+    any_, hbm, vmem, smem = (pl.BlockSpec(memory_space=m) for m in (pl.ANY, pltpu.HBM, pltpu.VMEM, pltpu.SMEM))
     dma = pltpu.SemaphoreType.DMA
     sent, cells = pltpu.VMEM((16, 16, 2, 128), F32), pltpu.VMEM((128, 2, 2, 128), F32)
     rows = pltpu.VMEM((256, 2, 128), F32)
@@ -417,48 +424,50 @@
         main_kernel,
         out_shape=(
             jax.ShapeDtypeStruct(planes, F32),
-            jax.ShapeDtypeStruct(spectral_weight.shape, F32),
+            jax.ShapeDtypeStruct(modes, F32),
             jax.ShapeDtypeStruct((GROUPS, 48, CH * NY), BF16),
             jax.ShapeDtypeStruct((8, 128), F32),
         ),
-        in_specs=[any_, any_, any_, vmem, smem, smem, vmem, vmem, vmem, vmem, any_, any_, any_, any_],
+        in_specs=[hbm] * 4 + [smem] * 2 + [hbm] * 8,
         out_specs=(any_, any_, vmem, vmem),
         scratch_shapes=[
             pltpu.VMEM(planes, BF16), pltpu.VMEM(planes, BF16), pltpu.VMEM(planes, BF16), pltpu.VMEM(planes, F32),
-            pltpu.VMEM((128, C, C), F32), pltpu.VMEM((C, 32, 128), F32), pltpu.VMEM((128, C, C), F32),
+            pltpu.VMEM(modes, F32), pltpu.VMEM((C, 32, 128), F32), pltpu.VMEM(modes, F32),
+            pltpu.VMEM((C, C), BF16), pltpu.VMEM((32, 256), BF16), pltpu.VMEM((16, 256), F32),
+            pltpu.VMEM((128, 48), BF16), pltpu.VMEM((128, 48), BF16),
             pltpu.VMEM((CH * NY, 256), BF16), pltpu.VMEM((2, 128, 256), F32),
             pltpu.VMEM((256, CH * NY), BF16), pltpu.VMEM((256, CH * NY), BF16),
             pltpu.VMEM((GROUPS, 16, 256), F32), pltpu.VMEM((GROUPS, 48, CH * NY), BF16), pltpu.VMEM((32, 128), F32),
             pltpu.VMEM((C * 16, C * 16), BF16), pltpu.VMEM((C * 16 + 16, C * 16), F32),
             sent, cells, sent, cells, rows, sent, rows, sent,
             pltpu.VMEM((8, 128), F32), small, pltpu.VMEM((8, 128), F32), small,
-            dma((9,)), dma((8,)), dma((1,)), dma((8,)), dma((4,)), dma((4,)), dma((2,)), dma((2,)),
+            dma((14,)), dma((1,)), dma((1,)), dma((1,)), dma((4,)), dma((4,)), dma((2,)), dma((2,)),
         ],
-        compiler_params=pltpu.CompilerParams(collective_id=0, has_side_effects=True, vmem_limit_bytes=56 * 2**20),
+        compiler_params=pltpu.CompilerParams(collective_id=0, has_side_effects=True, vmem_limit_bytes=57 * 2**20),
     )(
-        field.reshape(planes), cotangent.reshape(planes), spectral_weight, mix_weight, bias,
+        field.reshape(planes), cotangent.reshape(planes), weight, mix_weight, bias,
         tab["t_fwd"], tab["x_fwd"], tab["z_fwd"], tab["z_back"], tab["x_back"],
         tab["y_fwd"], tab["t_back"], tab["yb_high"], tab["yb_low"],
     )
-    whole = lambda *dims: pl.BlockSpec(dims, lambda k: (0,) * len(dims))
     field_grad, wg, bg, sg = pl.pallas_call(
         last_kernel,
-        grid=(GROUPS,),
+        grid=(TD,),
         out_shape=(
             jax.ShapeDtypeStruct(planes, BF16),
             jax.ShapeDtypeStruct((C, C), F32),
             jax.ShapeDtypeStruct((1, C), F32),
-            jax.ShapeDtypeStruct(spectral_weight.shape, F32),
+            jax.ShapeDtypeStruct(modes, F32),
         ),
         in_specs=[
-            pl.BlockSpec((CH, NX, NY), lambda k: (k, 0, 0)),
-            pl.BlockSpec((1, 48, CH * NY), lambda k: (k, 0, 0)),
+            pl.BlockSpec((C, NX, NY), lambda k: (k, 0, 0)),
+            pl.BlockSpec((2, 48, CH * NY), lambda k: (k, 0, 0)),
             whole(NX, 48), whole(8, 128), any_,
         ],
-        out_specs=(pl.BlockSpec((CH, NX, NY), lambda k: (k, 0, 0)), whole(C, C), whole(1, C), any_),
-        scratch_shapes=[dma(())],
-        compiler_params=pltpu.CompilerParams(vmem_limit_bytes=32 * 2**20),
+        out_specs=(pl.BlockSpec((C, NX, NY), lambda k: (k, 0, 0)), whole(C, C), whole(1, C), any_),
+        scratch_shapes=[pltpu.VMEM(modes, F32), dma((2,))],
+        compiler_params=pltpu.CompilerParams(vmem_limit_bytes=60 * 2**20),
     )(lin, h_rows, tab["x_back"], sums, sg)
+    sg = jnp.transpose(sg.reshape(TD, 16, C, 2, C), (0, 1, 3, 2, 4))
     return field_grad.reshape(shape), wg, bg.reshape(C), sg
 
 

time: 103 us -> 76.6 us (0.74)
  Pallas kernels: 91.8 us -> 75.8 us
  local copies, waits for them, and re-layouts: 10.1 us -> 0 us
    pallas_call x1, Pallas kernels: 87.5 us -> 69.4 us  [per_device(): pl.pallas_call(main_kernel, out_shape=(jax.ShapeDtypeStruct(planes, F32),...]
    unnamed x12 -> x0, local copies, waits for them, and re-layouts: 10.1 us -> none
    pallas_call x1, Pallas kernels: 4.31 us -> 6.37 us  [per_device(): pl.pallas_call(last_kernel, grid=(TD,), out_shape=(jax.ShapeDtypeStruct(p...]
where the time goes in v1:
time: 76.6 us; the launch traced here: 76.4 us
  Pallas kernels  75.8 us (99%)
    pallas_call x1, Pallas kernels, per_device(): pl.pallas_call(main_kernel, out_shape=(jax.ShapeDtypeStruct(planes, F32),...  69.4 us
    pallas_call x1, Pallas kernels, per_device(): pl.pallas_call(last_kernel, grid=(TD,), out_shape=(jax.ShapeDtypeStruct(p...  6.37 us

profile of v1, /device:TPU:1, one launch (start us, length us, event | category | flops | bytes accessed | tf_op | source)
XLA Modules:
  0.0 76.4 jit_solution(15390170299390247207)
XLA Ops:
  0.6 69.4 %shard_map.165 = (f32[80,128,128]{2,1,0:T(8,128)}, f32[64,20,2,20]{3,2,1,0:T(2,128)}, bf16[8,48,1280]{2,1,0:T(8,128)(2,1)}, f32[8,128]{1,0:T(8,128)}) custom-call(bf16[80,128,128]{2,1,0:T(8,128)(2,1)} %bitcast.12, bf16[80,128,128]{2,1,0:T(8,128)(2,1)} %bitcast.13, f32[64,20,2,20]{3,2,1,0:T(2,128)} %bitcast.14, bf16[20,20]{1,0:T(8,128)(2,1)} %mix_h.1, ...), custom_call_target="tpu_custom_call" | custom-call | tf_op jit(solution)/shard_map/pallas_call | solution.py:423
  70.1 6.4 %shard_map.166 = (bf16[80,128,128]{2,1,0:T(8,128)(2,1)}, f32[20,20]{1,0:T(8,128)}, f32[1,20]{1,0:T(1,128)}, f32[64,20,2,20]{3,2,1,0:T(2,128)}) custom-call(f32[80,128,128]{2,1,0:T(8,128)} %get-tuple-element.12.lin, bf16[8,48,1280]{2,1,0:T(8,128)(2,1)} %get-tuple-element.13.cells, bf16[128,48]{1,0:T(8,128)(2,1)} %constant.19.clone.z_back_h.x_back_h.x_back, ...), custom_call_target="tpu_custom_call" | custom-call | tf_op jit(solution)/shard_map/pallas_call | solution.py:452

commit v2 on v1

--- a/solution.py
+++ b/solution.py
@@ -67,7 +67,7 @@
 
 def gelu_slope(v):
     size = jnp.abs(v)
-    bell = jnp.exp(v * v * -0.5)
+    bell = jnp.exp2(v * v * -0.7213475204444817)
     d = 1.0 + 0.2316419 * size
     t = pl.reciprocal(d, approx=True)
     t = t * (2.0 - d * t)
@@ -110,9 +110,6 @@
     ]
     table_in = [load(4, y_fwd_h, y_fwd), load(9, x_fwd_h, x_fwd)]
     w_in = [pltpu.make_async_copy(weight_h, w_raw, w_sem.at[0])]
-    for copy in table_in + field_in + w_in + rest_in:
-        copy.start()
-
     barrier = pltpu.get_barrier_semaphore()
 
     steps = sorted(((dy, dx) for dy in range(4) for dx in range(4)), key=lambda d: -(min(d[0], 4 - d[0]) + min(d[1], 4 - d[1])))
@@ -156,11 +153,13 @@
     def by_cell(buffer):
         return lambda p, pz, c, t: buffer.at[p * 16 + pz * 2 + c, t]
 
-    def plane_modes(k, planes):
-        lhs = jnp.concatenate(planes, axis=1)
-        high, low = split(dot(lhs, y_fwd[...]))
-        both = dot(x_fwd[...], jnp.concatenate([high, low], axis=0))
-        xs[k] = both[:16] + both[16:]
+    def plane_modes(t, source):
+        halves = [[source[t * C + half * CH + i] for i in range(CH)] for half in range(2)]
+        y_done = dot(jnp.concatenate([jnp.concatenate(h, axis=1) for h in halves], axis=0), y_fwd[...])
+        for half in range(2):
+            high, low = split(y_done[half * NX : half * NX + NX])
+            both = dot(x_fwd[...], jnp.concatenate([high, low], axis=0))
+            xs[t * 2 + half] = both[:16] + both[16:]
 
     def mode_messages(send):
         parts = [xs[k] for k in range(GROUPS)]
@@ -245,14 +244,16 @@
         lax.fori_loop(0, 16, step, 0)
 
     each_peer(greet)
+    for copy in table_in + field_in + w_in + rest_in:
+        copy.start()
     for copy in table_in + field_in:
         copy.wait()
 
     def field_step(k, _):
-        plane_modes(k, [field[k * CH + i] for i in range(CH)])
+        plane_modes(k, field)
         return 0
 
-    lax.fori_loop(0, GROUPS, field_step, 0)
+    lax.fori_loop(0, TD, field_step, 0)
     mode_messages(send1)
     pl.semaphore_wait(barrier, 255)
     exchange(0, by_mode(send1), recv1.at[me])
@@ -278,20 +279,18 @@
     arrived(1, recv2)
     cell_rows(recv2, h_rows)
 
-    def grad_step(k, _):
-        planes = []
-        for n in range(5):
-            pair = dot(x_back[...], h_rows[k, :, n * 256 : n * 256 + 256])
-            for i in range(2):
-                p = k * CH + n * 2 + i
-                slope = gelu_slope(lin[p] + pair[:, i * 128 : i * 128 + 128])
-                value = (cot[p].astype(F32) * slope).astype(BF16)
-                grad[p] = value
-                planes.append(value)
-        plane_modes(k, planes)
+    def grad_step(t, _):
+        for half in range(2):
+            for n in range(5):
+                pair = dot(x_back[...], h_rows[t * 2 + half, :, n * 256 : n * 256 + 256])
+                for i in range(2):
+                    p = t * C + half * CH + n * 2 + i
+                    slope = gelu_slope(lin[p] + pair[:, i * 128 : i * 128 + 128])
+                    grad[p] = (cot[p].astype(F32) * slope).astype(BF16)
+        plane_modes(t, grad)
         return 0
 
-    lax.fori_loop(0, GROUPS, grad_step, 0)
+    lax.fori_loop(0, TD, grad_step, 0, unroll=2)
     mode_messages(send3)
     exchange(2, by_mode(send3), recv3.at[me])
 
@@ -378,34 +377,51 @@
         pltpu.make_async_copy(sent, sent, small_send.at[k]).wait()
 
 
-def last_kernel(lin, cells, x_back, sums, sg_in, out, wg, bg, sg_out, staged, sem):
-    k = pl.program_id(0)
-    copy_in = pltpu.make_async_copy(sg_in, staged, sem.at[0])
-    copy_out = pltpu.make_async_copy(staged, sg_out, sem.at[1])
-
-    @pl.when(k == 0)
-    def _():
-        copy_in.start()
-        scale = 1.0 / math.sqrt(NX * NY * NZ * NT)
-        rows = jnp.concatenate([sums[:, 32 * i : 32 * i + 32] for i in range(3)], axis=0) * scale
-        wg[...] = jnp.transpose(rows)[:C, :C]
-        bg[...] = rows[C : C + 1, :C]
-
-    for half in range(2):
+def last_kernel(
+    lin_h, cells_h, x_back_h, sums_h, sg_h, out_h, wg_h, bg_h, sg_out_h,
+    lin, cells, x_back, sums, staged, out, wg, bg, lin_sem, cells_sem, out_sem, sem,
+):
+    def part(k, n=1):
+        return pl.ds(k * n, n)
+
+    x_in = pltpu.make_async_copy(x_back_h, x_back, sem.at[0])
+    sums_in = pltpu.make_async_copy(sums_h, sums, sem.at[1])
+    sg_in = pltpu.make_async_copy(sg_h, staged, sem.at[2])
+    sg_out = pltpu.make_async_copy(staged, sg_out_h, sem.at[3])
+    wg_out = pltpu.make_async_copy(wg, wg_h, sem.at[4])
+    bg_out = pltpu.make_async_copy(bg, bg_h, sem.at[5])
+    cells_in = [pltpu.make_async_copy(cells_h.at[part(k)], cells.at[part(k)], cells_sem.at[k]) for k in range(GROUPS)]
+    lin_in = [pltpu.make_async_copy(lin_h.at[part(k, CH)], lin.at[part(k, CH)], lin_sem.at[k]) for k in range(GROUPS)]
+    field_out = [pltpu.make_async_copy(out.at[part(k, CH)], out_h.at[part(k, CH)], out_sem.at[k]) for k in range(GROUPS)]
+    x_in.start()
+    for k in range(GROUPS):
+        cells_in[k].start()
+        lin_in[k].start()
+        if k == 1:
+            sums_in.start()
+            sg_in.start()
+    x_in.wait()
+    for k in range(GROUPS):
+        cells_in[k].wait()
+        lin_in[k].wait()
         for n in range(5):
-            pair = dot(x_back[...], cells[half, :, n * 256 : n * 256 + 256])
+            pair = dot(x_back[...], cells[k, :, n * 256 : n * 256 + 256])
             for i in range(2):
-                p = half * CH + n * 2 + i
+                p = k * CH + n * 2 + i
                 out[p] = (lin[p] + pair[:, i * 128 : i * 128 + 128]).astype(BF16)
-
-    @pl.when(k == 1)
-    def _():
-        copy_in.wait()
-        copy_out.start()
-
-    @pl.when(k == pl.num_programs(0) - 1)
-    def _():
-        copy_out.wait()
+        field_out[k].start()
+        if k == 3:
+            sums_in.wait()
+            scale = 1.0 / math.sqrt(NX * NY * NZ * NT)
+            rows = jnp.concatenate([sums[:, 32 * i : 32 * i + 32] for i in range(3)], axis=0) * scale
+            wg[...] = jnp.transpose(rows)[:C, :C]
+            bg[...] = rows[C : C + 1, :C]
+            wg_out.start()
+            bg_out.start()
+            sg_in.wait()
+            sg_out.start()
+    for copy in [*field_out, wg_out, bg_out, sg_out]:
+        copy.wait()
 
 
 def per_device(field, cotangent, mix_weight, bias, spectral_weight):
@@ -414,7 +430,6 @@
     planes = (PLANES, NX, NY)
     weight = jnp.transpose(spectral_weight, (0, 1, 3, 2, 4)).reshape(64, C, 2, C)
     modes = (64, C, 2, C)
-    whole = lambda *dims: pl.BlockSpec(dims, lambda k: (0,) * len(dims))
     any_, hbm, vmem, smem = (pl.BlockSpec(memory_space=m) for m in (pl.ANY, pltpu.HBM, pltpu.VMEM, pltpu.SMEM))
     dma = pltpu.SemaphoreType.DMA
     sent, cells = pltpu.VMEM((16, 16, 2, 128), F32), pltpu.VMEM((128, 2, 2, 128), F32)
@@ -451,20 +466,20 @@
     )
     field_grad, wg, bg, sg = pl.pallas_call(
         last_kernel,
-        grid=(TD,),
         out_shape=(
             jax.ShapeDtypeStruct(planes, BF16),
             jax.ShapeDtypeStruct((C, C), F32),
             jax.ShapeDtypeStruct((1, C), F32),
             jax.ShapeDtypeStruct(modes, F32),
         ),
-        in_specs=[
-            pl.BlockSpec((C, NX, NY), lambda k: (k, 0, 0)),
-            pl.BlockSpec((2, 48, CH * NY), lambda k: (k, 0, 0)),
-            whole(NX, 48), whole(8, 128), any_,
+        in_specs=[any_] * 5,
+        out_specs=(any_,) * 4,
+        scratch_shapes=[
+            pltpu.VMEM(planes, F32), pltpu.VMEM((GROUPS, 48, CH * NY), BF16), pltpu.VMEM((NX, 48), BF16),
+            pltpu.VMEM((8, 128), F32), pltpu.VMEM(modes, F32), pltpu.VMEM(planes, BF16),
+            pltpu.VMEM((C, C), F32), pltpu.VMEM((1, C), F32),
+            dma((GROUPS,)), dma((GROUPS,)), dma((GROUPS,)), dma((6,)),
         ],
-        out_specs=(pl.BlockSpec((C, NX, NY), lambda k: (k, 0, 0)), whole(C, C), whole(1, C), any_),
-        scratch_shapes=[pltpu.VMEM(modes, F32), dma((2,))],
         compiler_params=pltpu.CompilerParams(vmem_limit_bytes=60 * 2**20),
     )(lin, h_rows, tab["x_back"], sums, sg)
     sg = jnp.transpose(sg.reshape(TD, 16, C, 2, C), (0, 1, 3, 2, 4))

time: 76.6 us -> 73.4 us (0.958)
  Pallas kernels: 75.8 us -> 72.6 us
    pallas_call x1, Pallas kernels: 69.4 us -> 67.6 us  [per_device(): pl.pallas_call(main_kernel, out_shape=(jax.ShapeDtypeStruct(planes, F32),...]
    pallas_call x1, Pallas kernels: 6.37 us -> 5 us  [per_device(): pl.pallas_call(last_kernel, out_shape=(jax.ShapeDtypeStruct(planes, BF16)...]
where the time goes in v2:
time: 73.4 us; the launch traced here: 73.3 us
  Pallas kernels  72.6 us (99%)
    pallas_call x1, Pallas kernels, per_device(): pl.pallas_call(main_kernel, out_shape=(jax.ShapeDtypeStruct(planes, F32),...  67.6 us
    pallas_call x1, Pallas kernels, per_device(): pl.pallas_call(last_kernel, out_shape=(jax.ShapeDtypeStruct(planes, BF16)...  5 us

profile of v2, /device:TPU:1, one launch (start us, length us, event | category | flops | bytes accessed | tf_op | source)
XLA Modules:
  0.0 73.3 jit_solution(15744819306254786020)
XLA Ops:
  0.6 67.6 %shard_map.165 = (f32[80,128,128]{2,1,0:T(8,128)}, f32[64,20,2,20]{3,2,1,0:T(2,128)}, bf16[8,48,1280]{2,1,0:T(8,128)(2,1)}, f32[8,128]{1,0:T(8,128)}) custom-call(bf16[80,128,128]{2,1,0:T(8,128)(2,1)} %bitcast.12, bf16[80,128,128]{2,1,0:T(8,128)(2,1)} %bitcast.13, f32[64,20,2,20]{3,2,1,0:T(2,128)} %bitcast.14, bf16[20,20]{1,0:T(8,128)(2,1)} %mix_h.1, ...), custom_call_target="tpu_custom_call" | custom-call | tf_op jit(solution)/shard_map/pallas_call | solution.py:438
  68.3 5.0 %shard_map.166 = (bf16[80,128,128]{2,1,0:T(8,128)(2,1)}, f32[20,20]{1,0:T(8,128)}, f32[1,20]{1,0:T(1,128)}, f32[64,20,2,20]{3,2,1,0:T(2,128)}) custom-call(f32[80,128,128]{2,1,0:T(8,128)} %get-tuple-element.12.lin_h, bf16[8,48,1280]{2,1,0:T(8,128)(2,1)} %get-tuple-element.13.cells_h, bf16[128,48]{1,0:T(8,128)(2,1)} %constant.19.clone.z_back_h.x_back_h, ...), custom_call_target="tpu_custom_call" | custom-call | tf_op jit(solution)/shard_map/pallas_call | solution.py:467

commit v3 on v2

--- a/solution.py
+++ b/solution.py
@@ -213,7 +213,8 @@
             for k in range(GROUPS):
                 out[k, 0:16, cut] = top[k * 16 : k * 16 + 16]
                 out[k, 16:32, cut] = rest[k * 16 : k * 16 + 16]
-                out[k, 32:48, cut] = top[k * 16 : k * 16 + 16]
+                if out.shape[1] == 48:
+                    out[k, 32:48, cut] = top[k * 16 : k * 16 + 16]
 
     def tile_rows(source, t, xt):
         at = pl.multiple_of(xt * 16, 16)
@@ -230,9 +231,8 @@
         same = lax.rem(lax.broadcasted_iota(jnp.int32, wide.shape, 0), 16) == lax.rem(lax.broadcasted_iota(jnp.int32, wide.shape, 1), 16)
         mix_kron[...] = jnp.where(same, wide, 0.0).astype(BF16)
 
-    def channel_mix(source, add_bias):
-        def step(k, _):
-            pair, xt = lax.rem(k, 2), k // 2
+    def channel_mix(source, pair, add_bias):
+        def step(xt, _):
             out = dot(mix_kron[...], pair_rows(source, pair, xt))
             at = pl.multiple_of(xt * 16, 16)
             for i in range(2):
@@ -241,7 +241,7 @@
                     lin[(pair * 2 + i) * C + o, pl.ds(at, 16), :] = part + bias[o] if add_bias else part
             return 0
 
-        lax.fori_loop(0, 16, step, 0)
+        lax.fori_loop(0, 8, step, 0)
 
     each_peer(greet)
     for copy in table_in + field_in + w_in + rest_in:
@@ -260,7 +260,8 @@
     for copy in rest_in + w_in:
         copy.wait()
     make_kron(False)
-    channel_mix(field, True)
+    for pair in range(2):
+        channel_mix(field, pair, True)
     w_t[...] = jnp.zeros_like(w_t)
     for o in range(C):
         turned = jnp.transpose(jnp.concatenate([w_raw[:, o, b, :] for b in range(2)], axis=0))
@@ -347,6 +348,11 @@
         return 0
 
     lax.fori_loop(1, 16, plane_step, 0)
+    half_planes = [pl.ds(pair * 2 * C, 2 * C) for pair in range(2)]
+    lin_out = [pltpu.make_async_copy(lin.at[at], lin_o.at[at], out_sem.at[pair]) for pair, at in enumerate(half_planes)]
+    for pair in range(2):
+        channel_mix(grad, pair, False)
+        lin_out[pair].start()
     for o in range(C):
         row = o if o < CH else o - CH + CP
         turned = jnp.transpose(field_spec * grad_spec[row : row + 1])
@@ -356,9 +362,6 @@
     sg_out = [pltpu.make_async_copy(sg_raw, sg_o, sg_sem.at[0])]
     for copy in sg_out:
         copy.start()
-    channel_mix(grad, False)
-    lin_out = pltpu.make_async_copy(lin, lin_o, out_sem.at[0])
-    lin_out.start()
     arrived(3, recv4)
     cell_rows(recv4, cells_o)
     pltpu.make_async_copy(plane_r, plane_r, small_recv.at[1]).wait()
@@ -366,9 +369,8 @@
     for i in range(1, 16):
         total = total + plane_r[i]
     sums_o[...] = total
-    for copy in sg_out:
+    for copy in sg_out + lin_out:
         copy.wait()
-    lin_out.wait()
     for k in range(4):
         sent = recv1.at[pl.ds(0, 255)]
         pltpu.make_async_copy(sent, sent, send_sem.at[k]).wait()
@@ -405,7 +407,8 @@
         cells_in[k].wait()
         lin_in[k].wait()
         for n in range(5):
-            pair = dot(x_back[...], cells[k, :, n * 256 : n * 256 + 256])
+            part_k = cells[k, :, n * 256 : n * 256 + 256]
+            pair = dot(x_back[...], jnp.concatenate([part_k, part_k[:16]], axis=0))
             for i in range(2):
                 p = k * CH + n * 2 + i
                 out[p] = (lin[p] + pair[:, i * 128 : i * 128 + 128]).astype(BF16)
@@ -440,7 +443,7 @@
         out_shape=(
             jax.ShapeDtypeStruct(planes, F32),
             jax.ShapeDtypeStruct(modes, F32),
-            jax.ShapeDtypeStruct((GROUPS, 48, CH * NY), BF16),
+            jax.ShapeDtypeStruct((GROUPS, 32, CH * NY), BF16),
             jax.ShapeDtypeStruct((8, 128), F32),
         ),
         in_specs=[hbm] * 4 + [smem] * 2 + [hbm] * 8,
@@ -456,7 +459,7 @@
             pltpu.VMEM((C * 16, C * 16), BF16), pltpu.VMEM((C * 16 + 16, C * 16), F32),
             sent, cells, sent, cells, rows, sent, rows, sent,
             pltpu.VMEM((8, 128), F32), small, pltpu.VMEM((8, 128), F32), small,
-            dma((14,)), dma((1,)), dma((1,)), dma((1,)), dma((4,)), dma((4,)), dma((2,)), dma((2,)),
+            dma((14,)), dma((1,)), dma((2,)), dma((1,)), dma((4,)), dma((4,)), dma((2,)), dma((2,)),
         ],
         compiler_params=pltpu.CompilerParams(collective_id=0, has_side_effects=True, vmem_limit_bytes=57 * 2**20),
     )(
@@ -475,7 +478,7 @@
         in_specs=[any_] * 5,
         out_specs=(any_,) * 4,
         scratch_shapes=[
-            pltpu.VMEM(planes, F32), pltpu.VMEM((GROUPS, 48, CH * NY), BF16), pltpu.VMEM((NX, 48), BF16),
+            pltpu.VMEM(planes, F32), pltpu.VMEM((GROUPS, 32, CH * NY), BF16), pltpu.VMEM((NX, 48), BF16),
             pltpu.VMEM((8, 128), F32), pltpu.VMEM(modes, F32), pltpu.VMEM(planes, BF16),
             pltpu.VMEM((C, C), F32), pltpu.VMEM((1, C), F32),
             dma((GROUPS,)), dma((GROUPS,)), dma((GROUPS,)), dma((6,)),

time: 73.4 us -> 73.4 us (level)
  no operation moved by 1% of the time
where the time goes in v3:
time: 73.4 us; the launch traced here: 73.3 us
  Pallas kernels  72.5 us (99%)
  between operations  0.8 us (1%)
    pallas_call x1, Pallas kernels, per_device(): pl.pallas_call(main_kernel, out_shape=(jax.ShapeDtypeStruct(planes, F32),...  67.5 us
    pallas_call x1, Pallas kernels, per_device(): pl.pallas_call(last_kernel, out_shape=(jax.ShapeDtypeStruct(planes, BF16)...  4.95 us

profile of v3, /device:TPU:1, one launch (start us, length us, event | category | flops | bytes accessed | tf_op | source)
XLA Modules:
  0.0 73.3 jit_solution(14841937211888069722)
XLA Ops:
  0.6 67.5 %shard_map.165 = (f32[80,128,128]{2,1,0:T(8,128)}, f32[64,20,2,20]{3,2,1,0:T(2,128)}, bf16[8,32,1280]{2,1,0:T(8,128)(2,1)}, f32[8,128]{1,0:T(8,128)}) custom-call(bf16[80,128,128]{2,1,0:T(8,128)(2,1)} %bitcast.12, bf16[80,128,128]{2,1,0:T(8,128)(2,1)} %bitcast.13, f32[64,20,2,20]{3,2,1,0:T(2,128)} %bitcast.14, bf16[20,20]{1,0:T(8,128)(2,1)} %mix_h.1, ...), custom_call_target="tpu_custom_call" | custom-call | tf_op jit(solution)/shard_map/pallas_call | solution.py:441
  68.1 5.0 %shard_map.166 = (bf16[80,128,128]{2,1,0:T(8,128)(2,1)}, f32[20,20]{1,0:T(8,128)}, f32[1,20]{1,0:T(1,128)}, f32[64,20,2,20]{3,2,1,0:T(2,128)}) custom-call(f32[80,128,128]{2,1,0:T(8,128)} %get-tuple-element.12.lin_h, bf16[8,32,1280]{2,1,0:T(8,128)(2,1)} %get-tuple-element.13.cells_h, bf16[128,48]{1,0:T(8,128)(2,1)} %constant.19.clone.z_back_h.x_back_h, ...), custom_call_target="tpu_custom_call" | custom-call | tf_op jit(solution)/shard_map/pallas_call | solution.py:470
